TPU v7x, 32 devices: a whole 2x2x4 slice. The times are simulated.
32 devices in a mesh: grp: 2 (over y), seq: 4 (over z), blk: 2 (over x), rep: 2 (over core).
Axes of the slice: x: 2, y: 2, z: 4, core: 2. Of those that a mesh axis runs over, the one named last changes fastest.
Arguments:
- q_proj: bfloat16 [8, 2048, 512], P(('grp', 'blk', 'rep'), 'seq'), parts along dimension 0, may hold values from -6 to 6
- k_proj: bfloat16 [8, 2048, 128], P(('grp', 'blk', 'rep'), 'seq'), parts along dimension 0, may hold values from -6 to 6
- v_proj: bfloat16 [8, 2048, 128], P(('grp', 'blk', 'rep'), 'seq'), parts along dimension 0, may hold values from -6 to 6
- q_gain: float32 [128], replicated, may hold values from 0.5 to 1.5
- k_gain: float32 [128], replicated, may hold values from 0.5 to 1.5
- out_weight: bfloat16 [512, 2560], P('seq'), may hold values from -0.25 to 0.25
- lengths: int32 [8, 1], P(('grp', 'blk', 'rep')), parts along dimension 0, may hold values from 512 to 2048, as said below
- query_emb: bfloat16 [512, 2560], P(('grp', 'blk')), parts along dimension 0, may hold values from -6 to 6
- teacher: float32 [512, 4], P(('grp', 'blk')), parts along dimension 0, may hold values from -16 to 16
Outputs:
- q_grad: bfloat16 [8, 2048, 512], P(('grp', 'blk', 'rep'), 'seq'), parts along dimension 0
- k_grad: bfloat16 [8, 2048, 128], P(('grp', 'blk', 'rep'), 'seq'), parts along dimension 0
- v_grad: bfloat16 [8, 2048, 128], P(('grp', 'blk', 'rep'), 'seq'), parts along dimension 0
- weight_grad: bfloat16 [1024, 2560], P(('grp', 'seq')), parts along dimension 0
- row_loss: float32 [512], P(('grp', 'blk')), parts along dimension 0
- col_loss: float32 [8], P('grp'), parts along dimension 0
There are 2 independent parts, one for each index of `grp`. A program takes and returns all parts, laid end to end along the dimension named above; an argument that names none is the same for every part. Nothing has to cross between parts.
Inputs may be any that keep to these rules, and one draw needn't show every extreme that they name: `lengths`: live tokens of each passage, counted from its first position; the rest is padding.
All inputs are finite; a program needn't handle non-finite values.
Results may differ from a plain program's by a relative error of at most 0.017.
Values may be sent and summed in bfloat16 or wider, within the bound.
A program may use at most 64 MiB of HBM per device.

v0:
```python
import math
import jax
import jax.numpy as jnp
from jax import lax
from jax.sharding import PartitionSpec as P

HD = 128
PASS_LEN = 2048
logit_divisor = 0.05


def rms_scale(wide):
    return lax.rsqrt(jnp.mean(wide * wide, axis=-1, keepdims=True) + 1e-06)


def normed(source, gain_weights):
    wide = source.astype(jnp.float32)
    return (wide * rms_scale(wide) * gain_weights).astype(jnp.bfloat16)


def norm_back(source, gain_weights, grad_out):
    wide = source.astype(jnp.float32)
    inv_rms = rms_scale(wide)
    scaled_grad = gain_weights * grad_out
    return (
        inv_rms * scaled_grad
        - wide * inv_rms**3 * jnp.mean(scaled_grad * wide, axis=-1, keepdims=True)
    ).astype(jnp.bfloat16)


def shards(q_proj, k_proj, v_proj, q_gain, k_gain, out_weight, lengths, query_emb, teacher):
    number_of_sequences = lax.axis_size("seq")
    blk_count = lax.axis_size("blk")
    tok_dev = q_proj.shape[1]
    heads_all = q_proj.shape[2] // HD
    kv_heads = k_proj.shape[2] // HD
    group_size = heads_all // kv_heads
    local_heads = out_weight.shape[0] // HD
    group_tok = tok_dev * number_of_sequences
    passes = group_tok // PASS_LEN
    pass_lens = lengths[0]
    inv_root = 1.0 / math.sqrt(HD)
    block_rows = min(512, PASS_LEN)
    block_count = PASS_LEN // block_rows

    def widen(rows):
        spread = jnp.broadcast_to(
            rows.reshape(tok_dev, kv_heads, 1, HD), (tok_dev, kv_heads, group_size, HD)
        )
        return spread.reshape(tok_dev, heads_all * HD)

    q_heads, k_heads, v_heads = (
        lax.all_to_all(q_proj[0], "seq", split_axis=1, concat_axis=0, tiled=True),
        lax.all_to_all(widen(k_proj[0]), "seq", split_axis=1, concat_axis=0, tiled=True),
        lax.all_to_all(widen(v_proj[0]), "seq", split_axis=1, concat_axis=0, tiled=True),
    )
    head_shape = (passes, PASS_LEN, local_heads, HD)
    q_raw = q_heads.reshape(head_shape)
    k_raw = k_heads.reshape(head_shape)
    v_all = v_heads.reshape(head_shape)
    q_unit = normed(q_raw, q_gain)
    k_unit = normed(k_raw, k_gain)
    positions = lax.iota(jnp.int32, PASS_LEN)
    passage = 0
    q_block = q_unit[passage]
    k_block = k_unit[passage]
    stored = []
    for attend_index in range(block_count):
        attend_ending = (attend_index + 1) * block_rows
        rows_here = q_block[attend_index * block_rows : attend_ending]
        logits = (
            jnp.einsum(
                "thd,uhd->htu",
                rows_here,
                k_block[:attend_ending],
                preferred_element_type=jnp.float32,
            )
            * inv_root
        )
        causal = (attend_index * block_rows + lax.iota(jnp.int32, block_rows))[:, None] >= lax.iota(
            jnp.int32, attend_ending
        )[None, :]
        powers = jnp.where(causal[None], jnp.exp(logits), 0.0)
        stored.append(
            lax.optimization_barrier(
                (powers / jnp.sum(powers, axis=2, keepdims=True)).astype(jnp.bfloat16)
            )
        )
    blocks = stored
    saved_blocks = [blocks]
    live_len = pass_lens[passage]
    live_mask = (positions < live_len).astype(jnp.bfloat16)
    col_weight = jnp.zeros((local_heads, PASS_LEN), jnp.float32)
    for index in range(block_count):
        ending = (index + 1) * block_rows
        column_part = jnp.einsum(
            "t,htu->hu",
            live_mask[index * block_rows : ending],
            blocks[index],
            preferred_element_type=jnp.float32,
        )
        col_weight = col_weight.at[:, :ending].add(column_part)
    col_weight = col_weight / live_len.astype(jnp.float32)
    pooled_list = [jnp.sum(col_weight.T[:, :, None] * v_all[passage].astype(jnp.float32), axis=0)]
    weight_list = [col_weight.astype(jnp.bfloat16)]
    pooled = jnp.stack(pooled_list)
    col_weights = jnp.stack(weight_list)
    pooled_flat = pooled.reshape(passes, local_heads * HD).astype(jnp.bfloat16)
    partial_value = jnp.dot(pooled_flat, out_weight, preferred_element_type=jnp.float32)
    summed = lax.psum(partial_value, "seq")
    inv_norm = lax.rsqrt(jnp.sum(summed * summed, axis=1, keepdims=True) + 1e-06)
    passage_unit = summed * inv_norm
    passage_all = lax.all_gather(
        passage_unit.astype(jnp.bfloat16), ("blk", "rep"), axis=0, tiled=True
    )
    query_wide = query_emb.astype(jnp.float32)
    request_unit_length = (
        query_wide * lax.rsqrt(jnp.sum(query_wide * query_wide, axis=1, keepdims=True) + 1e-06)
    ).astype(jnp.bfloat16)
    learner_similarities = (
        lax.dot_general(
            request_unit_length,
            passage_all,
            (((1,), (1,)), ((), ())),
            preferred_element_type=jnp.float32,
        )
        / logit_divisor
    )
    exp_student = jnp.exp(learner_similarities)
    exp_teacher = jnp.exp(teacher)
    row_student = jnp.sum(exp_student, axis=1, keepdims=True)
    row_teacher = jnp.sum(exp_teacher, axis=1, keepdims=True)
    gap = exp_teacher * (teacher - learner_similarities)
    col_student, col_teacher, col_gap = lax.psum(
        (jnp.sum(exp_student, axis=0), jnp.sum(exp_teacher, axis=0), jnp.sum(gap, axis=0)), "blk"
    )
    row_loss = (
        jnp.sum(gap, axis=1) / row_teacher[:, 0]
        - jnp.log(row_teacher[:, 0])
        + jnp.log(row_student[:, 0])
    )
    col_loss = col_gap / col_teacher - jnp.log(col_teacher) + jnp.log(col_student)
    query_total = query_emb.shape[0] * blk_count
    passage_total = teacher.shape[1]
    similarity_derivative = (
        (exp_student / row_student - exp_teacher / row_teacher) / query_total
        + (exp_student / col_student - exp_teacher / col_teacher) / passage_total
    ).astype(jnp.bfloat16)
    grad_block = lax.psum_scatter(
        (
            lax.dot_general(
                similarity_derivative,
                request_unit_length,
                (((0,), (0,)), ((), ())),
                preferred_element_type=jnp.float32,
            )
            / logit_divisor
        ).astype(jnp.bfloat16),
        "blk",
        scatter_dimension=0,
        tiled=True,
    ).astype(jnp.float32)
    representation_derivative = lax.dynamic_slice_in_dim(
        grad_block, lax.axis_index("rep") * passes, passes, 0
    )
    grad_sum = (
        (
            representation_derivative
            - passage_unit
            * jnp.sum(passage_unit * representation_derivative, axis=1, keepdims=True)
        )
        * inv_norm
    ).astype(jnp.bfloat16)
    pooled_every, grads_every = (
        lax.all_gather(pooled_flat, ("blk", "rep"), axis=0, tiled=True),
        lax.all_gather(grad_sum, ("blk", "rep"), axis=0, tiled=True),
    )
    weight_grad = lax.dot_general(
        pooled_every, grads_every, (((0,), (0,)), ((), ())), preferred_element_type=jnp.float32
    ).astype(jnp.bfloat16)
    grad_pool = lax.dot_general(
        grad_sum, out_weight, (((1,), (1,)), ((), ())), preferred_element_type=jnp.float32
    )
    pool_heads = grad_pool.reshape(passes, local_heads, HD)
    passage = 0
    blocks = saved_blocks[passage]
    q_block = q_unit[passage]
    k_block = k_unit[passage]
    live_len = pass_lens[passage]
    live_mask = (positions < live_len).astype(jnp.float32) / live_len.astype(jnp.float32)
    value_dot = jnp.sum(v_all[passage].astype(jnp.float32) * pool_heads[passage][None], axis=2).T
    grad_k_copy = jnp.zeros((PASS_LEN, local_heads, HD), jnp.float32)
    query_parts = []
    for index in range(block_count):
        ending = (index + 1) * block_rows
        stored_block = blocks[index]
        value_here = value_dot[:, None, :ending]
        mean_dot = jnp.sum(stored_block.astype(jnp.float32) * value_here, axis=2)
        local_live_mask = live_mask[index * block_rows : ending]
        grad_logits = (
            stored_block.astype(jnp.float32)
            * local_live_mask[None, :, None]
            * (value_here - mean_dot[:, :, None])
            * inv_root
        ).astype(jnp.bfloat16)
        query_parts.append(
            jnp.einsum(
                "htu,uhd->thd", grad_logits, k_block[:ending], preferred_element_type=jnp.float32
            )
        )
        key_part = jnp.einsum(
            "htu,thd->uhd",
            grad_logits,
            q_block[index * block_rows : ending],
            preferred_element_type=jnp.float32,
        )
        grad_k_copy = grad_k_copy.at[:ending].add(key_part)
    grad_q_unit = jnp.concatenate(query_parts, axis=0)
    q_list = [norm_back(q_raw[passage], q_gain, grad_q_unit)]
    k_list = [norm_back(k_raw[passage], k_gain, grad_k_copy)]
    q_terms = jnp.stack(q_list)
    k_terms = jnp.stack(k_list)
    flat_shape = (group_tok, local_heads * HD)

    def narrow(terms):
        wide = terms.astype(jnp.float32).reshape(tok_dev, kv_heads, group_size, HD)
        return jnp.sum(wide, axis=2).astype(jnp.bfloat16).reshape(tok_dev, kv_heads * HD)

    q_back, k_back, v_back = (
        lax.all_to_all(q_terms.reshape(flat_shape), "seq", split_axis=0, concat_axis=1, tiled=True),
        lax.all_to_all(k_terms.reshape(flat_shape), "seq", split_axis=0, concat_axis=1, tiled=True),
        lax.all_to_all(
            (col_weights.astype(jnp.float32).transpose(0, 2, 1)[..., None] * pool_heads[:, None])
            .astype(jnp.bfloat16)
            .reshape(flat_shape),
            "seq",
            split_axis=0,
            concat_axis=1,
            tiled=True,
        ),
    )
    k_out = narrow(k_back)
    v_out = narrow(v_back)
    return (q_back[None], k_out[None], v_out[None], weight_grad, row_loss, col_loss)


def solution(mesh):
    placed = (
        P(("grp", "blk", "rep"), "seq", None),
        P(("grp", "blk", "rep"), "seq", None),
        P(("grp", "blk", "rep"), "seq", None),
        P(),
        P(),
        P("seq", None),
        P(("grp", "blk", "rep"), None),
        P(("grp", "blk"), None),
        P(("grp", "blk"), None),
    )
    return jax.shard_map(
        shards,
        mesh=mesh,
        in_specs=placed,
        out_specs=(
            P(("grp", "blk", "rep"), "seq", None),
            P(("grp", "blk", "rep"), "seq", None),
            P(("grp", "blk", "rep"), "seq", None),
            P(("grp", "seq"), None),
            P(("grp", "blk")),
            P("grp"),
        ),
        check_vma=False,
    )
```

profile of v0, /device:TPU:0, one launch (start us, length us, event | category | flops | bytes accessed | tf_op | source)
XLA Modules:
  0.0 180.6 jit_solution(1321558911935933446)
XLA Ops:
  0.7 1.1 copy.44
  1.8 0.8 broadcast_in_dim.25
  2.7 6.3 %all-to-all-start.1 = ((bf16[512,4,128]{0,2,1:T(8,128)(2,1)}), bf16[512,4,128]{0,2,1:T(8,128)(2,1)S(1)}, u32[]{:S(2)}, u32[]{:S(2)}) async-start(bf16[512,4,128]{0,2,1:T(8,128)(2,1)} %broadcast_in_dim.25), calls=%async_computation.1 | async-start | bytes 1048576 | tf_op jit(solution)/shard_map/all_to_all | solution.py:54
  9.0 1.0 copy.42
  10.7 12.7 %all-to-all-done.1 = bf16[512,4,128]{0,2,1:T(8,128)(2,1)S(1)} async-done(((bf16[512,4,128]{0,2,1:T(8,128)(2,1)}), bf16[512,4,128]{0,2,1:T(8,128)(2,1)S(1)}, u32[]{:S(2)}, u32[]{:S(2)}) %all-to-all-start.1) | async-done | bytes 524320 | tf_op jit(solution)/shard_map/all_to_all | solution.py:54
  23.5 3.5 %all-to-all-start = ((bf16[512,4,128]{0,2,1:T(8,128)(2,1)}), bf16[512,4,128]{0,2,1:T(8,128)(2,1)S(1)}, u32[]{:S(2)}, u32[]{:S(2)}) async-start(bf16[512,4,128]{0,2,1:T(8,128)(2,1)} %bitcast), calls=%async_computation | async-start | bytes 1048576 | tf_op jit(solution)/shard_map/all_to_all | solution.py:53
  31.1 9.8 %all-to-all-done = bf16[512,4,128]{0,2,1:T(8,128)(2,1)S(1)} async-done(((bf16[512,4,128]{0,2,1:T(8,128)(2,1)}), bf16[512,4,128]{0,2,1:T(8,128)(2,1)S(1)}, u32[]{:S(2)}, u32[]{:S(2)}) %all-to-all-start) | async-done | bytes 524320 | tf_op jit(solution)/shard_map/all_to_all | solution.py:53
  40.9 0.9 broadcast_in_dim.29
  41.8 4.3 %all-to-all-start.2 = ((bf16[512,4,128]{2,0,1:T(8,128)(2,1)}), bf16[512,4,128]{2,0,1:T(8,128)(2,1)}, u32[]{:S(2)}, u32[]{:S(2)}) async-start(bf16[512,4,128]{2,0,1:T(8,128)(2,1)} %broadcast_in_dim.29), calls=%async_computation.2 | async-start | bytes 1048576 | tf_op jit(solution)/shard_map/all_to_all | solution.py:55
  47.9 1.4 fusion.96
  52.5 1.0 fusion.99
  54.9 0.9 fusion.35
  55.8 1.0 fusion.16
  56.8 1.0 convert_reduce_fusion
  57.8 2.3 %all-to-all-done.2 = bf16[512,4,128]{2,0,1:T(8,128)(2,1)} async-done(((bf16[512,4,128]{2,0,1:T(8,128)(2,1)}), bf16[512,4,128]{2,0,1:T(8,128)(2,1)}, u32[]{:S(2)}, u32[]{:S(2)}) %all-to-all-start.2) | async-done | bytes 524320 | tf_op jit(solution)/shard_map/all_to_all | solution.py:55
  60.1 1.1 convert_element_type.407
  61.2 1.0 copy-done.11
  63.3 16.8 %psum.28 = f32[1,2560]{1,0:T(1,128)S(1)} all-reduce(f32[1,2560]{1,0:T(1,128)S(1)} %fusion.77), channel_id=1, replica_groups=mesh['grp'=2,'seq'=4,'blk'=2,'rep'=2] {'seq'}, use_global_device_ids=true, to_apply=%region_11.12 | all-reduce | flops 2560 | bytes 20480 | tf_op jit(solution)/shard_map/psum | solution.py:110
  81.4 5.2 %all-gather.1 = bf16[4,1,2560]{2,1,0:T(2,128)(2,1)S(1)} all-gather(bf16[1,1,2560]{2,1,0:T(2,128)(2,1)S(1)} %convert_bitcast_fusion.1), channel_id=1, replica_groups=mesh['grp'=2,'seq'=4,'blk'=2,'rep'=2] {'blk','rep'}, dimensions={0}, use_global_device_ids=true | all-gather | bytes 25600 | tf_op jit(solution)/shard_map/all_gather | solution.py:113
  86.6 2.0 %fusion.80 = (f32[4]{0:T(128)S(1)}, f32[128]{0:T(128)}, f32[4]{0:T(128)S(1)}, f32[128]{0:T(128)S(1)}, f32[4]{0:T(128)S(1)}, /*index=5*/f32[128]{0:T(128)S(1)}, f32[128,4]{0,1:T(4,128)S(1)}) fusion(f32[128,4]{0,1:T(4,128)S(1)} %copy-done.55, bf16[4,1,2560]{2,1,0:T(2,128)(2,1)S(1)} %all-gather.1, bf16[128,2560]{1,0:T(8,128)(2,1)} %param.36, ...), kind=kOutput, calls=%fused_computation.165 | convolution fusion | flops 3608692 | bytes 682032 | tf_op jit(solution)/shard_map/dot_general | solution.py:121
  88.6 5.4 %all-reduce.3 = (f32[4]{0:T(128)S(1)}, f32[4]{0:T(128)S(1)}, f32[4]{0:T(128)}) all-reduce(f32[4]{0:T(128)S(1)} %get-tuple-element.140, f32[4]{0:T(128)S(1)} %get-tuple-element.138, f32[4]{0:T(128)S(1)} %get-tuple-element.136), channel_id=1, replica_groups=mesh['grp'=2,'seq'=4,'blk'=2,'rep'=2] {'blk'}, use_global_device_ids=true, to_apply=%region_18.19 | all-reduce | flops 12 | bytes 96 | tf_op jit(solution)/shard_map/psum | solution.py:134
  94.1 1.4 fusion.4
  95.5 8.3 %all-reduce.2 = bf16[4,2560]{1,0:T(4,128)(2,1)S(1)} all-reduce(bf16[4,2560]{1,0:T(4,128)(2,1)S(1)} %fusion.4), channel_id=3, replica_groups=mesh['grp'=2,'seq'=4,'blk'=2,'rep'=2] {'blk'}, use_global_device_ids=true, to_apply=%region_19.20.clone | all-reduce | flops 10240 | bytes 40960
  105.9 1.6 fusion.44
  108.6 2.1 %convolution_bitcast_fusion.3 = f32[512,1,128]{0,2,1:T(8,128)} fusion(bf16[1,2048,1,128]{3,1,2,0:T(8,128)(2,1)} %copy-done.19, bf16[1,512,512]{1,2,0:T(8,128)(2,1)S(1)} %fusion.55, f32[512]{0:T(512)S(1)} %fusion.39, f32[512]{0:T(512)S(1)} %bitcast.270, f32[512]{0:T(512)S(1)} %get-tuple-element.148), kind=kOutput, calls=%fused_computation.61 | convolution fusion | flops 68681728 | bytes 923648 | tf_op jit(solution)/shard_map/htu,thd->uhd/dot_general | solution.py:211
  112.0 1.3 fusion.87
  113.3 0.9 copy-done.8
  114.9 0.9 fusion.56
  117.3 1.1 pad_maximum_fusion
  118.4 2.5 %copy.54 = f32[2048,128]{1,0:T(8,128)} copy(f32[2048,128]{0,1:T(8,128)} %pad_maximum_fusion) | data formatting | bytes 2097152 | tf_op jit(solution)/shard_map/concatenate | solution.py:218
  120.9 1.3 copy.55
  122.3 1.6 fusion.42
  123.9 2.9 %fusion.49 = bf16[4,512,128]{2,1,0:T(8,128)(2,1)} fusion(f32[4,512,128]{2,1,0:T(8,128)} %bitcast.241, bf16[512,4,128]{2,0,1:T(8,128)(2,1)} %copy-done.15, f32[4,512]{1,0:T(4,128)S(1)} %div.160, f32[4,512]{1,0:T(4,128)} %get-tuple-element.147, f32[128]{0:T(128)} %param.32, f32[4,512]{1,0:T(4,128)} %get-tuple-element.145), kind=kLoop, calls=%fused_computation.86 | loop fusion | flops 1835008 | bytes 2122240 | tf_op jit(solution)/shard_map/convert_element_type | solution.py:28
  126.8 2.1 %copy.48 = bf16[4,512,128]{1,2,0:T(8,128)(2,1)} copy(bf16[4,512,128]{2,1,0:T(8,128)(2,1)} %fusion.49) | data formatting | bytes 1048576 | tf_op jit(solution)/shard_map/convert_element_type | solution.py:28
  128.9 4.1 %all-to-all-start.3 = ((bf16[4,512,128]{1,2,0:T(8,128)(2,1)}), bf16[4,512,128]{1,2,0:T(8,128)(2,1)}, u32[]{:S(2)}, u32[]{:S(2)}) async-start(bf16[4,512,128]{1,2,0:T(8,128)(2,1)} %copy.48), calls=%async_computation.3 | async-start | bytes 1048576 | tf_op jit(solution)/shard_map/all_to_all | solution.py:230
  133.1 1.3 copy.56
  134.5 2.0 %fusion.33 = f32[2048,1,128]{0,2,1:T(8,128)S(1)} fusion(f32[2048,1,128]{0,2,1:T(8,128)S(1)} %scatter-add.25, bf16[1,2048,1,128]{3,1,2,0:T(8,128)(2,1)} %copy-done.19, bf16[1,512,1024]{2,1,0:T(8,128)(2,1)} %copy-done.12, f32[512]{0:T(512)} %copy-done.41, f32[1024]{0:T(1024)} %bitcast.267, f32[512]{0:T(512)} %get-tuple-element.151), kind=kOutput, calls=%fused_computation.60 | convolution fusion | flops 137494528 | bytes 2236416 | tf_op jit(solution)/shard_map/htu,thd->uhd/dot_general | solution.py:211
  136.5 0.9 fusion.12
  139.6 0.9 copy.50
  140.5 4.7 %all-to-all-done.3 = bf16[4,512,128]{1,2,0:T(8,128)(2,1)} async-done(((bf16[4,512,128]{1,2,0:T(8,128)(2,1)}), bf16[4,512,128]{1,2,0:T(8,128)(2,1)}, u32[]{:S(2)}, u32[]{:S(2)}) %all-to-all-start.3) | async-done | bytes 524320 | tf_op jit(solution)/shard_map/all_to_all | solution.py:230
  145.2 3.5 %all-to-all-start.4 = ((bf16[4,512,128]{1,2,0:T(8,128)(2,1)}), bf16[4,512,128]{1,2,0:T(8,128)(2,1)S(1)}, u32[]{:S(2)}, u32[]{:S(2)}) async-start(bf16[4,512,128]{1,2,0:T(8,128)(2,1)} %copy.50), calls=%async_computation.4 | async-start | bytes 1048576 | tf_op jit(solution)/shard_map/all_to_all | solution.py:231
  148.7 1.1 multiply_convert_fusion
  149.8 11.1 %all-to-all-done.4 = bf16[4,512,128]{1,2,0:T(8,128)(2,1)S(1)} async-done(((bf16[4,512,128]{1,2,0:T(8,128)(2,1)}), bf16[4,512,128]{1,2,0:T(8,128)(2,1)S(1)}, u32[]{:S(2)}, u32[]{:S(2)}) %all-to-all-start.4) | async-done | bytes 524320 | tf_op jit(solution)/shard_map/all_to_all | solution.py:231
  160.9 3.5 %all-to-all-start.5 = ((bf16[4,512,128]{2,1,0:T(8,128)(2,1)}), bf16[4,512,128]{2,1,0:T(8,128)(2,1)S(1)}, u32[]{:S(2)}, u32[]{:S(2)}) async-start(bf16[4,512,128]{2,1,0:T(8,128)(2,1)} %multiply_convert_fusion), calls=%async_computation.5 | async-start | bytes 1048576 | tf_op jit(solution)/shard_map/all_to_all | solution.py:232
  164.4 5.0 %all-gather.2 = bf16[4,1,128]{2,1,0:T(2,128)(2,1)S(1)} all-gather(bf16[1,1,128]{2,1,0:T(2,128)(2,1)S(1)} %bitcast.273), channel_id=2, replica_groups=mesh['grp'=2,'seq'=4,'blk'=2,'rep'=2] {'blk','rep'}, dimensions={0}, use_global_device_ids=true | all-gather | bytes 1280 | tf_op jit(solution)/shard_map/all_gather | solution.py:175
  169.4 5.2 %all-gather.3 = bf16[4,1,2560]{2,1,0:T(2,128)(2,1)S(1)} all-gather(bf16[1,1,2560]{2,1,0:T(2,128)(2,1)S(1)} %bitcast.262), channel_id=1, replica_groups=mesh['grp'=2,'seq'=4,'blk'=2,'rep'=2] {'blk','rep'}, dimensions={0}, use_global_device_ids=true | all-gather | bytes 25600 | tf_op jit(solution)/shard_map/all_gather | solution.py:176
  175.7 1.2 convolution_convert_fusion
  176.9 2.0 %copy.52 = bf16[1,512,512]{2,1,0:T(8,128)(2,1)} copy(bf16[1,512,512]{1,2,0:T(8,128)(2,1)} %bitcast.63) | data formatting | bytes 1048576
  (181 shorter events, 22.8 us)
Async XLA Ops:
  0.6 62.5 %copy-start = (bf16[128,2560]{1,0:T(8,128)(2,1)S(1)}, bf16[128,2560]{1,0:T(8,128)(2,1)}, u32[]{:S(2)}) copy-start(bf16[128,2560]{1,0:T(8,128)(2,1)} %param.34) | copy-start | bytes 1966084
  0.6 26.4 %copy-start.56 = (u32[32]{0:T(128)S(1)}, u32[32]{0:T(128)}, u32[]{:S(2)}) copy-start(u32[32]{0:T(128)} %constant.272) | copy-start | bytes 388
  0.7 8.3 %copy-start.22 = (bf16[1,512,512]{2,1,0:T(8,128)(2,1)S(1)}, bf16[1,512,512]{2,1,0:T(8,128)(2,1)}, u32[]{:S(2)}) copy-start(bf16[1,512,512]{2,1,0:T(8,128)(2,1)} %param.29) | copy-start | bytes 1572868
  0.7 28.9 %copy-start.21 = (bf16[128,2560]{1,0:T(8,128)(2,1)S(1)}, bf16[128,2560]{1,0:T(8,128)(2,1)}, u32[]{:S(2)}) copy-start(bf16[128,2560]{1,0:T(8,128)(2,1)} %param.36) | copy-start | bytes 1966084
  2.7 20.8 %all-to-all-start.1 = ((bf16[512,4,128]{0,2,1:T(8,128)(2,1)}), bf16[512,4,128]{0,2,1:T(8,128)(2,1)S(1)}, u32[]{:S(2)}, u32[]{:S(2)}) async-start(bf16[512,4,128]{0,2,1:T(8,128)(2,1)} %broadcast_in_dim.25), calls=%async_computation.1 | async-start | bytes 1048576 | tf_op jit(solution)/shard_map/all_to_all | solution.py:54
  23.5 17.4 %all-to-all-start = ((bf16[512,4,128]{0,2,1:T(8,128)(2,1)}), bf16[512,4,128]{0,2,1:T(8,128)(2,1)S(1)}, u32[]{:S(2)}, u32[]{:S(2)}) async-start(bf16[512,4,128]{0,2,1:T(8,128)(2,1)} %bitcast), calls=%async_computation | async-start | bytes 1048576 | tf_op jit(solution)/shard_map/all_to_all | solution.py:53
  26.9 14.0 %copy-start.26 = (bf16[1,512,128]{2,1,0:T(8,128)(2,1)S(1)}, bf16[1,512,128]{2,1,0:T(8,128)(2,1)}, u32[]{:S(2)}) copy-start(bf16[1,512,128]{2,1,0:T(8,128)(2,1)} %param.31) | copy-start | bytes 393220
  30.7 17.1 %copy-start.3 = (f32[512,4,128]{2,0,1:T(8,128)}, f32[512,4,128]{2,0,1:T(8,128)S(1)}, u32[]{:S(2)}) copy-start(f32[512,4,128]{2,0,1:T(8,128)S(1)} %convert_element_type.405) | copy-start | bytes 3145732
  41.8 5.8 %copy-start.31 = (f32[128]{0:T(128)S(1)}, f32[128]{0:T(128)}, u32[]{:S(2)}) copy-start(f32[128]{0:T(128)} %param.32) | copy-start | bytes 1540
  41.8 18.3 %all-to-all-start.2 = ((bf16[512,4,128]{2,0,1:T(8,128)(2,1)}), bf16[512,4,128]{2,0,1:T(8,128)(2,1)}, u32[]{:S(2)}, u32[]{:S(2)}) async-start(bf16[512,4,128]{2,0,1:T(8,128)(2,1)} %broadcast_in_dim.29), calls=%async_computation.2 | async-start | bytes 1048576 | tf_op jit(solution)/shard_map/all_to_all | solution.py:55
  46.3 3.0 %copy-start.15 = (bf16[512,4,128]{2,0,1:T(8,128)(2,1)}, bf16[512,4,128]{2,0,1:T(8,128)(2,1)S(1)}, u32[]{:S(2)}) copy-start(bf16[512,4,128]{2,0,1:T(8,128)(2,1)S(1)} %copy.43) | copy-start | bytes 1572868
  47.9 4.5 %copy-start.19 = (bf16[1,2048,1,128]{3,1,2,0:T(8,128)(2,1)}, bf16[1,2048,1,128]{3,1,2,0:T(8,128)(2,1)S(1)}, u32[]{:S(2)}) copy-start(bf16[1,2048,1,128]{3,1,2,0:T(8,128)(2,1)S(1)} %multiply_convert_fusion.2) | copy-start | bytes 1572868
  52.4 2.4 %copy-start.12 = (bf16[1,512,1024]{2,1,0:T(8,128)(2,1)}, bf16[1,512,1024]{2,1,0:T(8,128)(2,1)S(1)}, u32[]{:S(2)}) copy-start(bf16[1,512,1024]{2,1,0:T(8,128)(2,1)S(1)} %fusion.50) | copy-start | bytes 3145732
  53.9 1.9 %copy-start.7 = (bf16[1,512,1536]{2,1,0:T(8,128)(2,1)}, bf16[1,512,1536]{2,1,0:T(8,128)(2,1)S(1)}, u32[]{:S(2)}) copy-start(bf16[1,512,1536]{2,1,0:T(8,128)(2,1)S(1)} %fusion.27) | copy-start | bytes 4718596
  57.8 28.9 %copy-start.55 = (f32[128,4]{0,1:T(4,128)S(1)}, f32[128,4]{0,1:T(4,128)}, u32[]{:S(2)}) copy-start(f32[128,4]{0,1:T(4,128)} %param.37) | copy-start | bytes 6148
  88.6 19.3 %copy-start.46 = (f32[128]{0:T(128)}, f32[128]{0:T(128)S(1)}, u32[]{:S(2)}) copy-start(f32[128]{0:T(128)S(1)} %get-tuple-element.139) | copy-start | bytes 1540
  88.6 19.3 %copy-start.48 = (f32[128]{0:T(128)}, f32[128]{0:T(128)S(1)}, u32[]{:S(2)}) copy-start(f32[128]{0:T(128)S(1)} %get-tuple-element.141) | copy-start | bytes 1540
  94.1 9.7 %copy-start.50 = (f32[4]{0:T(128)}, f32[4]{0:T(128)S(1)}, u32[]{:S(2)}) copy-start(f32[4]{0:T(128)S(1)} %get-tuple-element.142) | copy-start | bytes 52
  94.1 9.7 %copy-start.52 = (f32[4]{0:T(128)}, f32[4]{0:T(128)S(1)}, u32[]{:S(2)}) copy-start(f32[4]{0:T(128)S(1)} %get-tuple-element.143) | copy-start | bytes 52
  105.0 3.1 %copy-start.27 = (bf16[1,2560]{1,0:T(2,128)(2,1)}, bf16[1,2560]{1,0:T(2,128)(2,1)S(1)}, u32[]{:S(2)}) copy-start(bf16[1,2560]{1,0:T(2,128)(2,1)S(1)} %subtract_multiply_fusion) | copy-start | bytes 15364
  105.1 3.1 %copy-start.24 = (bf16[1,2048,1,128]{3,1,2,0:T(8,128)(2,1)S(1)}, bf16[1,2048,1,128]{3,1,2,0:T(8,128)(2,1)}, u32[]{:S(2)}) copy-start(bf16[1,2048,1,128]{3,1,2,0:T(8,128)(2,1)} %copy-done.23) | copy-start | bytes 1572868
  108.0 7.9 %copy-start.30 = (f32[1,1024]{1,0:T(1,128)}, f32[1,1024]{1,0:T(1,128)S(1)}, u32[]{:S(2)}) copy-start(f32[1,1024]{1,0:T(1,128)S(1)} %slice.261) | copy-start | bytes 12292
  108.6 7.9 %copy-start.16 = (f32[128,512]{1,0:T(8,128)}, f32[128,512]{1,0:T(8,128)S(1)}, u32[]{:S(2)}) copy-start(f32[128,512]{1,0:T(8,128)S(1)} %fusion.60) | copy-start | bytes 786436
  112.0 2.6 %copy-start.1 = (bf16[512,2048]{1,0:T(8,128)(2,1)}, bf16[512,2048]{1,0:T(8,128)(2,1)S(1)}, u32[]{:S(2)}) copy-start(bf16[512,2048]{1,0:T(8,128)(2,1)S(1)} %fusion.22) | copy-start | bytes 6291460
  112.0 2.2 %copy-start.8 = (bf16[1,512,1536]{2,1,0:T(8,128)(2,1)S(1)}, bf16[1,512,1536]{2,1,0:T(8,128)(2,1)}, u32[]{:S(2)}) copy-start(bf16[1,512,1536]{2,1,0:T(8,128)(2,1)} %copy-done.7) | copy-start | bytes 4718596
  112.0 2.6 %copy-start.13 = (bf16[1,512,1024]{2,1,0:T(8,128)(2,1)S(1)}, bf16[1,512,1024]{2,1,0:T(8,128)(2,1)}, u32[]{:S(2)}) copy-start(bf16[1,512,1024]{2,1,0:T(8,128)(2,1)} %copy-done.12) | copy-start | bytes 3145732
  117.3 3.7 %copy-start.10 = (f32[512,4,128]{2,0,1:T(8,128)S(1)}, f32[512,4,128]{2,0,1:T(8,128)}, u32[]{:S(2)}) copy-start(f32[512,4,128]{2,0,1:T(8,128)} %copy-done.9) | copy-start | bytes 3145732
  123.9 9.2 %copy-start.6 = (f32[512,4,128]{2,0,1:T(8,128)S(1)}, f32[512,4,128]{2,0,1:T(8,128)}, u32[]{:S(2)}) copy-start(f32[512,4,128]{2,0,1:T(8,128)} %copy-done.3) | copy-start | bytes 3145732
  126.8 7.6 %copy-start.25 = (f32[512,1,128]{0,2,1:T(8,128)S(1)}, f32[512,1,128]{0,2,1:T(8,128)}, u32[]{:S(2)}) copy-start(f32[512,1,128]{0,2,1:T(8,128)} %convolution_bitcast_fusion.3) | copy-start | bytes 786436
  128.9 16.3 %all-to-all-start.3 = ((bf16[4,512,128]{1,2,0:T(8,128)(2,1)}), bf16[4,512,128]{1,2,0:T(8,128)(2,1)}, u32[]{:S(2)}, u32[]{:S(2)}) async-start(bf16[4,512,128]{1,2,0:T(8,128)(2,1)} %copy.48), calls=%async_computation.3 | async-start | bytes 1048576 | tf_op jit(solution)/shard_map/all_to_all | solution.py:230
  134.4 2.1 %copy-start.20 = (bf16[1,2048,1,128]{3,1,2,0:T(8,128)(2,1)S(1)}, bf16[1,2048,1,128]{3,1,2,0:T(8,128)(2,1)}, u32[]{:S(2)}) copy-start(bf16[1,2048,1,128]{3,1,2,0:T(8,128)(2,1)} %copy-done.19) | copy-start | bytes 1572868
  134.4 2.1 %copy-start.40 = (f32[512]{0:T(512)S(1)}, f32[512]{0:T(512)}, u32[]{:S(2)}) copy-start(f32[512]{0:T(512)} %copy-done.39) | copy-start | bytes 6148
  134.4 2.1 %copy-start.43 = (f32[512]{0:T(512)S(1)}, f32[512]{0:T(512)}, u32[]{:S(2)}) copy-start(f32[512]{0:T(512)} %get-tuple-element.150) | copy-start | bytes 6148
  136.5 1.6 copy-start.2
  136.5 1.8 %copy-start.14 = (f32[2048,1,128]{0,2,1:T(8,128)S(1)}, f32[2048,1,128]{0,2,1:T(8,128)}, u32[]{:S(2)}) copy-start(f32[2048,1,128]{0,2,1:T(8,128)} %copy.56) | copy-start | bytes 3145732
  136.5 1.8 %copy-start.34 = (f32[128]{0:T(128)S(1)}, f32[128]{0:T(128)}, u32[]{:S(2)}) copy-start(f32[128]{0:T(128)} %param.33) | copy-start | bytes 1540
  139.1 9.6 %copy-start.29 = (f32[2048]{0:T(1024)S(1)}, f32[2048]{0:T(1024)}, u32[]{:S(2)}) copy-start(f32[2048]{0:T(1024)} %get-tuple-element.167) | copy-start | bytes 24580
  139.1 9.6 %copy-start.36 = (f32[128]{0:T(128)S(1)}, f32[128]{0:T(128)}, u32[]{:S(2)}) copy-start(f32[128]{0:T(128)} %copy-done.35) | copy-start | bytes 1540
  139.5 24.9 %copy-start.38 = (bf16[128]{0:T(256)(128)(2,1)S(1)}, bf16[128]{0:T(256)(128)(2,1)}, u32[]{:S(2)}) copy-start(bf16[128]{0:T(256)(128)(2,1)} %copy-done.37) | copy-start | bytes 772
  139.5 29.9 %copy-start.28 = (bf16[1,2560]{1,0:T(2,128)(2,1)S(1)}, bf16[1,2560]{1,0:T(2,128)(2,1)}, u32[]{:S(2)}) copy-start(bf16[1,2560]{1,0:T(2,128)(2,1)} %copy-done.27) | copy-start | bytes 15364
  139.5 35.1 %copy-start.45 = (f32[128]{0:T(128)S(1)}, f32[128]{0:T(128)}, u32[]{:S(2)}) copy-start(f32[128]{0:T(128)} %get-tuple-element.137) | copy-start | bytes 1540
  139.6 35.1 %copy-start.47 = (f32[128]{0:T(128)S(1)}, f32[128]{0:T(128)}, u32[]{:S(2)}) copy-start(f32[128]{0:T(128)} %copy-done.46) | copy-start | bytes 1540
  139.6 35.1 %copy-start.49 = (f32[128]{0:T(128)S(1)}, f32[128]{0:T(128)}, u32[]{:S(2)}) copy-start(f32[128]{0:T(128)} %copy-done.48) | copy-start | bytes 1540
  139.6 35.6 %copy-start.51 = (f32[4]{0:T(128)S(1)}, f32[4]{0:T(128)}, u32[]{:S(2)}) copy-start(f32[4]{0:T(128)} %copy-done.50) | copy-start | bytes 52
  139.6 35.6 %copy-start.53 = (f32[4]{0:T(128)S(1)}, f32[4]{0:T(128)}, u32[]{:S(2)}) copy-start(f32[4]{0:T(128)} %copy-done.52) | copy-start | bytes 52
  139.6 35.6 %copy-start.54 = (f32[4]{0:T(128)S(1)}, f32[4]{0:T(128)}, u32[]{:S(2)}) copy-start(f32[4]{0:T(128)} %get-tuple-element.144) | copy-start | bytes 52
  145.2 15.7 %all-to-all-start.4 = ((bf16[4,512,128]{1,2,0:T(8,128)(2,1)}), bf16[4,512,128]{1,2,0:T(8,128)(2,1)S(1)}, u32[]{:S(2)}, u32[]{:S(2)}) async-start(bf16[4,512,128]{1,2,0:T(8,128)(2,1)} %copy.50), calls=%async_computation.4 | async-start | bytes 1048576 | tf_op jit(solution)/shard_map/all_to_all | solution.py:231
  160.9 18.9 %all-to-all-start.5 = ((bf16[4,512,128]{2,1,0:T(8,128)(2,1)}), bf16[4,512,128]{2,1,0:T(8,128)(2,1)S(1)}, u32[]{:S(2)}, u32[]{:S(2)}) async-start(bf16[4,512,128]{2,1,0:T(8,128)(2,1)} %multiply_convert_fusion), calls=%async_computation.5 | async-start | bytes 1048576 | tf_op jit(solution)/shard_map/all_to_all | solution.py:232
  (15 other events, 15.4 us)
where the time goes:
time: 182 us; the launch traced here: 181 us
  blocking collectives  46 us (25%)
  waiting for transfers between devices  40.6 us (22%)
  starting transfers between devices  25.1 us (14%)
  local copies, waits for them, and re-layouts  23 us (13%)
  other arithmetic  21.8 us (12%)
  matrix products  20.4 us (11%)
  between operations  3.64 us (2%)
    psum x1, blocking collectives, shards(): summed = lax.psum(partial_value, 'seq')  16.8 us
    all_to_all x1, waiting for transfers between devices, shards(): lax.all_to_all(widen(k_proj[0]), 'seq', split_axis=1, concat_axis=0, tile...  12.7 us
    all_to_all x1, waiting for transfers between devices, shards(): lax.all_to_all(k_terms.reshape(flat_shape), 'seq', split_axis=0, concat_a...  11.1 us
    unnamed x120, local copies, waits for them, and re-layouts  10.3 us
    all_to_all x1, waiting for transfers between devices, shards(): lax.all_to_all(q_proj[0], 'seq', split_axis=1, concat_axis=0, tiled=True)  9.79 us
    unnamed x1, blocking collectives  8.26 us
    all_to_all x1, starting transfers between devices, shards(): lax.all_to_all(widen(k_proj[0]), 'seq', split_axis=1, concat_axis=0, tile...  6.32 us
    dot_general x4, matrix products, shards(): jnp.einsum('htu,thd->uhd', grad_logits, q_block[index * block_rows:ending...  5.53 us
  transfers between devices with their start and end apart: 6, of which 5 were waited for; matrix products, arithmetic and copies ran while one was open for 15% of the time, Pallas kernels for 0%

commit v1 on v0

--- a/solution.py
+++ b/solution.py
@@ -7,6 +7,29 @@
 HD = 128
 PASS_LEN = 2048
 logit_divisor = 0.05
+
+
+def in_blocks(x, dim, size):
+    shape = x.shape
+    blocks = x.reshape(*shape[:dim], size, shape[dim] // size, *shape[dim + 1 :])
+    return jnp.moveaxis(blocks, dim, 0)
+
+
+def laid_out(parts, dim):
+    parts = jnp.moveaxis(parts, 0, dim)
+    shape = parts.shape
+    return parts.reshape(*shape[:dim], shape[dim] * shape[dim + 1], *shape[dim + 2 :])
+
+
+def exchange_in_pairs(array, axis, split_dim, concat_dim):
+    size, position = (lax.axis_size(axis), lax.axis_index(axis))
+    blocks = in_blocks(array, split_dim, size)
+    outs = [blocks[position]]
+    for hop in range(1, size):
+        sent = blocks[position ^ hop]
+        outs.append(lax.ppermute(sent, axis, [(i, i ^ hop) for i in range(size)]))
+    blocks = jnp.stack(outs)[position ^ jnp.arange(size)]
+    return laid_out(blocks, concat_dim)
 
 
 def rms_scale(wide):
@@ -228,7 +251,7 @@
 
     q_back, k_back, v_back = (
         lax.all_to_all(q_terms.reshape(flat_shape), "seq", split_axis=0, concat_axis=1, tiled=True),
-        lax.all_to_all(k_terms.reshape(flat_shape), "seq", split_axis=0, concat_axis=1, tiled=True),
+        exchange_in_pairs(k_terms.reshape(flat_shape), "seq", 0, 1),
         lax.all_to_all(
             (col_weights.astype(jnp.float32).transpose(0, 2, 1)[..., None] * pool_heads[:, None])
             .astype(jnp.bfloat16)

time: 182 us -> 178 us (0.978)
  waiting for transfers between devices: 40.6 us -> 33.3 us
  starting transfers between devices: 25.1 us -> 27.7 us
  other arithmetic: 21.8 us -> 23.8 us
    all_to_all x1 -> x0, waiting for transfers between devices: 11.1 us -> none  [shards(): lax.all_to_all(k_terms.reshape(flat_shape), 'seq', split_axis=0, concat_a...]
    all_to_all x1, waiting for transfers between devices: 0.01 us -> 9.04 us  [shards(): lax.all_to_all((col_weights.astype(jnp.float32).transpose(0, 2, 1)[..., N...]
    all_to_all x1, waiting for transfers between devices: 4.71 us -> 0.01 us  [shards(): lax.all_to_all(q_terms.reshape(flat_shape), 'seq', split_axis=0, concat_a...]
    ppermute x0 -> x3, starting transfers between devices: none -> 4.47 us  [exchange_in_pairs(): outs.append(lax.ppermute(sent, axis, [(i, i ^ hop) for i in range(size)]))]
    all_to_all x1 -> x0, starting transfers between devices: 3.47 us -> none  [shards(): lax.all_to_all(k_terms.reshape(flat_shape), 'seq', split_axis=0, concat_a...]
    unnamed x120 -> x121, local copies, waits for them, and re-layouts: 10.3 us -> 9.67 us
  transfers between devices with their start and end apart: 6 -> 8, of which waited for: 5 -> 4; matrix products, arithmetic and copies ran while one was open for 15% -> 16% of each run, Pallas kernels for 0% -> 0%
where the time goes in v1:
time: 178 us; the launch traced here: 177 us
  blocking collectives  46 us (26%)
  waiting for transfers between devices  33.3 us (19%)
  starting transfers between devices  27.7 us (16%)
  other arithmetic  23.8 us (13%)
  local copies, waits for them, and re-layouts  22.2 us (12%)
  matrix products  20.4 us (11%)
  between operations  3.62 us (2%)
    psum x1, blocking collectives, shards(): summed = lax.psum(partial_value, 'seq')  16.8 us
    all_to_all x1, waiting for transfers between devices, shards(): lax.all_to_all(widen(k_proj[0]), 'seq', split_axis=1, concat_axis=0, tile...  12.1 us
    all_to_all x1, waiting for transfers between devices, shards(): lax.all_to_all(q_proj[0], 'seq', split_axis=1, concat_axis=0, tiled=True)  9.77 us
    unnamed x121, local copies, waits for them, and re-layouts  9.67 us
    all_to_all x1, waiting for transfers between devices, shards(): lax.all_to_all((col_weights.astype(jnp.float32).transpose(0, 2, 1)[..., N...  9.04 us
    unnamed x1, blocking collectives  8.26 us
    all_to_all x1, starting transfers between devices, shards(): lax.all_to_all(widen(k_proj[0]), 'seq', split_axis=1, concat_axis=0, tile...  6.32 us
    dot_general x4, matrix products, shards(): jnp.einsum('htu,thd->uhd', grad_logits, q_block[index * block_rows:ending...  5.54 us
  transfers between devices with their start and end apart: 8, of which 4 were waited for; matrix products, arithmetic and copies ran while one was open for 16% of the time, Pallas kernels for 0%

profile of v1, /device:TPU:0, one launch (start us, length us, event | category | flops | bytes accessed | tf_op | source)
XLA Modules:
  0.0 176.9 jit_solution(9903260493630148989)
XLA Ops:
  0.7 1.1 copy.50
  1.8 0.8 broadcast_in_dim.25
  2.7 6.3 %all-to-all-start.1 = ((bf16[512,4,128]{0,2,1:T(8,128)(2,1)}), bf16[512,4,128]{0,2,1:T(8,128)(2,1)S(1)}, u32[]{:S(2)}, u32[]{:S(2)}) async-start(bf16[512,4,128]{0,2,1:T(8,128)(2,1)} %broadcast_in_dim.25), calls=%async_computation.1 | async-start | bytes 1048576 | tf_op jit(solution)/shard_map/all_to_all | solution.py:77
  9.0 1.0 copy.48
  11.3 12.1 %all-to-all-done.1 = bf16[512,4,128]{0,2,1:T(8,128)(2,1)S(1)} async-done(((bf16[512,4,128]{0,2,1:T(8,128)(2,1)}), bf16[512,4,128]{0,2,1:T(8,128)(2,1)S(1)}, u32[]{:S(2)}, u32[]{:S(2)}) %all-to-all-start.1) | async-done | bytes 524320 | tf_op jit(solution)/shard_map/all_to_all | solution.py:77
  23.5 3.5 %all-to-all-start = ((bf16[512,4,128]{0,2,1:T(8,128)(2,1)}), bf16[512,4,128]{0,2,1:T(8,128)(2,1)S(1)}, u32[]{:S(2)}, u32[]{:S(2)}) async-start(bf16[512,4,128]{0,2,1:T(8,128)(2,1)} %bitcast), calls=%async_computation | async-start | bytes 1048576 | tf_op jit(solution)/shard_map/all_to_all | solution.py:76
  31.1 9.8 %all-to-all-done = bf16[512,4,128]{0,2,1:T(8,128)(2,1)S(1)} async-done(((bf16[512,4,128]{0,2,1:T(8,128)(2,1)}), bf16[512,4,128]{0,2,1:T(8,128)(2,1)S(1)}, u32[]{:S(2)}, u32[]{:S(2)}) %all-to-all-start) | async-done | bytes 524320 | tf_op jit(solution)/shard_map/all_to_all | solution.py:76
  40.9 0.9 broadcast_in_dim.29
  41.8 4.3 %all-to-all-start.2 = ((bf16[512,4,128]{2,0,1:T(8,128)(2,1)}), bf16[512,4,128]{2,0,1:T(8,128)(2,1)}, u32[]{:S(2)}, u32[]{:S(2)}) async-start(bf16[512,4,128]{2,0,1:T(8,128)(2,1)} %broadcast_in_dim.29), calls=%async_computation.2 | async-start | bytes 1048576 | tf_op jit(solution)/shard_map/all_to_all | solution.py:78
  47.9 1.4 fusion.97
  52.4 1.0 fusion.100
  54.8 0.9 fusion.35
  55.8 1.0 fusion.16
  56.7 1.0 convert_reduce_fusion
  57.7 2.4 %all-to-all-done.2 = bf16[512,4,128]{2,0,1:T(8,128)(2,1)} async-done(((bf16[512,4,128]{2,0,1:T(8,128)(2,1)}), bf16[512,4,128]{2,0,1:T(8,128)(2,1)}, u32[]{:S(2)}, u32[]{:S(2)}) %all-to-all-start.2) | async-done | bytes 524320 | tf_op jit(solution)/shard_map/all_to_all | solution.py:78
  60.1 1.1 convert_element_type.407
  61.2 1.0 copy-done.11
  63.3 16.8 %psum.28 = f32[1,2560]{1,0:T(1,128)S(1)} all-reduce(f32[1,2560]{1,0:T(1,128)S(1)} %fusion.78), channel_id=1, replica_groups=mesh['grp'=2,'seq'=4,'blk'=2,'rep'=2] {'seq'}, use_global_device_ids=true, to_apply=%region_11.12 | all-reduce | flops 2560 | bytes 20480 | tf_op jit(solution)/shard_map/psum | solution.py:133
  81.5 5.2 %all-gather.1 = bf16[4,1,2560]{2,1,0:T(2,128)(2,1)S(1)} all-gather(bf16[1,1,2560]{2,1,0:T(2,128)(2,1)S(1)} %convert_bitcast_fusion.1), channel_id=1, replica_groups=mesh['grp'=2,'seq'=4,'blk'=2,'rep'=2] {'blk','rep'}, dimensions={0}, use_global_device_ids=true | all-gather | bytes 25600 | tf_op jit(solution)/shard_map/all_gather | solution.py:136
  86.7 2.0 %fusion.81 = (f32[4]{0:T(128)S(1)}, f32[128]{0:T(128)}, f32[4]{0:T(128)S(1)}, f32[128]{0:T(128)S(1)}, f32[4]{0:T(128)S(1)}, /*index=5*/f32[128]{0:T(128)S(1)}, f32[128,4]{0,1:T(4,128)S(1)}) fusion(f32[128,4]{0,1:T(4,128)S(1)} %copy-done.56, bf16[4,1,2560]{2,1,0:T(2,128)(2,1)S(1)} %all-gather.1, bf16[128,2560]{1,0:T(8,128)(2,1)} %param.36, ...), kind=kOutput, calls=%fused_computation.174 | convolution fusion | flops 3608692 | bytes 682032 | tf_op jit(solution)/shard_map/dot_general | solution.py:144
  88.6 5.4 %all-reduce.3 = (f32[4]{0:T(128)S(1)}, f32[4]{0:T(128)S(1)}, f32[4]{0:T(128)}) all-reduce(f32[4]{0:T(128)S(1)} %get-tuple-element.140, f32[4]{0:T(128)S(1)} %get-tuple-element.138, f32[4]{0:T(128)S(1)} %get-tuple-element.136), channel_id=1, replica_groups=mesh['grp'=2,'seq'=4,'blk'=2,'rep'=2] {'blk'}, use_global_device_ids=true, to_apply=%region_18.19 | all-reduce | flops 12 | bytes 96 | tf_op jit(solution)/shard_map/psum | solution.py:157
  94.1 1.4 fusion.4
  95.5 8.3 %all-reduce.2 = bf16[4,2560]{1,0:T(4,128)(2,1)S(1)} all-reduce(bf16[4,2560]{1,0:T(4,128)(2,1)S(1)} %fusion.4), channel_id=3, replica_groups=mesh['grp'=2,'seq'=4,'blk'=2,'rep'=2] {'blk'}, use_global_device_ids=true, to_apply=%region_19.20.clone | all-reduce | flops 10240 | bytes 40960
  105.9 1.6 fusion.44
  108.7 2.1 %convolution_bitcast_fusion.3 = f32[512,1,128]{0,2,1:T(8,128)} fusion(bf16[1,2048,1,128]{3,1,2,0:T(8,128)(2,1)} %copy-done.19, bf16[1,512,512]{1,2,0:T(8,128)(2,1)S(1)} %fusion.55, f32[512]{0:T(512)S(1)} %fusion.39, f32[512]{0:T(512)S(1)} %bitcast.284, f32[512]{0:T(512)S(1)} %get-tuple-element.152), kind=kOutput, calls=%fused_computation.62 | convolution fusion | flops 68681728 | bytes 923648 | tf_op jit(solution)/shard_map/htu,thd->uhd/dot_general | solution.py:234
  111.4 0.8 fusion.22
  112.6 1.3 fusion.88
  113.9 0.9 copy-done.8
  115.5 0.9 fusion.56
  117.9 1.1 pad_maximum_fusion
  119.0 2.5 %copy.61 = f32[2048,128]{1,0:T(8,128)} copy(f32[2048,128]{0,1:T(8,128)} %pad_maximum_fusion) | data formatting | bytes 2097152 | tf_op jit(solution)/shard_map/concatenate | solution.py:241
  121.5 1.3 copy.62
  122.9 1.6 fusion.42
  124.5 2.9 %fusion.49 = bf16[4,512,128]{2,1,0:T(8,128)(2,1)} fusion(f32[4,512,128]{2,1,0:T(8,128)} %bitcast.251, bf16[512,4,128]{2,0,1:T(8,128)(2,1)} %copy-done.15, f32[4,512]{1,0:T(4,128)S(1)} %div.160, f32[4,512]{1,0:T(4,128)} %get-tuple-element.151, f32[128]{0:T(128)} %param.32, f32[4,512]{1,0:T(4,128)} %get-tuple-element.149), kind=kLoop, calls=%fused_computation.87 | loop fusion | flops 1835008 | bytes 2122240 | tf_op jit(solution)/shard_map/convert_element_type | solution.py:51
  127.4 2.1 %copy.54 = bf16[4,512,128]{1,2,0:T(8,128)(2,1)} copy(bf16[4,512,128]{2,1,0:T(8,128)(2,1)} %fusion.49) | data formatting | bytes 1048576 | tf_op jit(solution)/shard_map/convert_element_type | solution.py:51
  129.5 4.2 %all-to-all-start.3 = ((bf16[4,512,128]{1,2,0:T(8,128)(2,1)}), bf16[4,512,128]{1,2,0:T(8,128)(2,1)}, u32[]{:S(2)}, u32[]{:S(2)}) async-start(bf16[4,512,128]{1,2,0:T(8,128)(2,1)} %copy.54), calls=%async_computation.3 | async-start | bytes 1048576 | tf_op jit(solution)/shard_map/all_to_all | solution.py:253
  133.7 1.3 copy.63
  135.1 2.0 %fusion.33 = f32[2048,1,128]{0,2,1:T(8,128)S(1)} fusion(f32[2048,1,128]{0,2,1:T(8,128)S(1)} %scatter-add.25, bf16[1,2048,1,128]{3,1,2,0:T(8,128)(2,1)} %copy-done.19, bf16[1,512,1024]{2,1,0:T(8,128)(2,1)} %copy-done.12, f32[512]{0:T(512)} %copy-done.42, f32[1024]{0:T(1024)} %bitcast.281, f32[512]{0:T(512)} %get-tuple-element.155), kind=kOutput, calls=%fused_computation.61 | convolution fusion | flops 137494528 | bytes 2236416 | tf_op jit(solution)/shard_map/htu,thd->uhd/dot_general | solution.py:234
  137.2 0.9 fusion.12
  140.3 3.8 %collective-permute-start.2 = (bf16[512,128]{1,0:T(8,128)(2,1)S(1)}, bf16[512,128]{1,0:T(8,128)(2,1)S(1)}, u32[]{:S(2)}, u32[]{:S(2)}) collective-permute-start(bf16[512,128]{1,0:T(8,128)(2,1)S(1)} %get-tuple-element.146), channel_id=1, source_target_pairs={{0,12},{4,8},{8,4},{12,0},{1,13},{5,9},{9,5},{13,1},{2,14},{6,10},... | collective-permute-start | bytes 393224 | tf_op jit(solution)/shard_map/ppermute | solution.py:30
  144.8 5.0 %all-gather.2 = bf16[4,1,128]{2,1,0:T(2,128)(2,1)S(1)} all-gather(bf16[1,1,128]{2,1,0:T(2,128)(2,1)S(1)} %bitcast.287), channel_id=2, replica_groups=mesh['grp'=2,'seq'=4,'blk'=2,'rep'=2] {'blk','rep'}, dimensions={0}, use_global_device_ids=true | all-gather | bytes 1280 | tf_op jit(solution)/shard_map/all_gather | solution.py:198
  149.9 5.2 %all-gather.3 = bf16[4,1,2560]{2,1,0:T(2,128)(2,1)S(1)} all-gather(bf16[1,1,2560]{2,1,0:T(2,128)(2,1)S(1)} %bitcast.276), channel_id=1, replica_groups=mesh['grp'=2,'seq'=4,'blk'=2,'rep'=2] {'blk','rep'}, dimensions={0}, use_global_device_ids=true | all-gather | bytes 25600 | tf_op jit(solution)/shard_map/all_gather | solution.py:199
  155.1 1.1 multiply_convert_fusion
  156.2 5.0 %all-to-all-start.4 = ((bf16[4,512,128]{2,1,0:T(8,128)(2,1)}), bf16[4,512,128]{2,1,0:T(8,128)(2,1)S(1)}, u32[]{:S(2)}, u32[]{:S(2)}) async-start(bf16[4,512,128]{2,1,0:T(8,128)(2,1)} %multiply_convert_fusion), calls=%async_computation.4 | async-start | bytes 1048576 | tf_op jit(solution)/shard_map/all_to_all | solution.py:255
  161.7 1.2 convolution_convert_fusion
  163.6 0.8 gather_fusion
  165.1 2.0 %copy.60 = bf16[1,512,512]{2,1,0:T(8,128)(2,1)} copy(bf16[1,512,512]{1,2,0:T(8,128)(2,1)} %bitcast.63) | data formatting | bytes 1048576
  167.2 9.0 %all-to-all-done.4 = bf16[4,512,128]{2,1,0:T(8,128)(2,1)S(1)} async-done(((bf16[4,512,128]{2,1,0:T(8,128)(2,1)}), bf16[4,512,128]{2,1,0:T(8,128)(2,1)S(1)}, u32[]{:S(2)}, u32[]{:S(2)}) %all-to-all-start.4) | async-done | bytes 524320 | tf_op jit(solution)/shard_map/all_to_all | solution.py:255
  (190 shorter events, 23.9 us)
Async XLA Ops:
  0.6 62.5 %copy-start = (bf16[128,2560]{1,0:T(8,128)(2,1)S(1)}, bf16[128,2560]{1,0:T(8,128)(2,1)}, u32[]{:S(2)}) copy-start(bf16[128,2560]{1,0:T(8,128)(2,1)} %param.34) | copy-start | bytes 1966084
  0.6 26.4 %copy-start.57 = (u32[32]{0:T(128)S(1)}, u32[32]{0:T(128)}, u32[]{:S(2)}) copy-start(u32[32]{0:T(128)} %constant.285) | copy-start | bytes 388
  0.7 8.3 %copy-start.22 = (bf16[1,512,512]{2,1,0:T(8,128)(2,1)S(1)}, bf16[1,512,512]{2,1,0:T(8,128)(2,1)}, u32[]{:S(2)}) copy-start(bf16[1,512,512]{2,1,0:T(8,128)(2,1)} %param.29) | copy-start | bytes 1572868
  0.7 28.9 %copy-start.21 = (bf16[128,2560]{1,0:T(8,128)(2,1)S(1)}, bf16[128,2560]{1,0:T(8,128)(2,1)}, u32[]{:S(2)}) copy-start(bf16[128,2560]{1,0:T(8,128)(2,1)} %param.36) | copy-start | bytes 1966084
  2.7 20.8 %all-to-all-start.1 = ((bf16[512,4,128]{0,2,1:T(8,128)(2,1)}), bf16[512,4,128]{0,2,1:T(8,128)(2,1)S(1)}, u32[]{:S(2)}, u32[]{:S(2)}) async-start(bf16[512,4,128]{0,2,1:T(8,128)(2,1)} %broadcast_in_dim.25), calls=%async_computation.1 | async-start | bytes 1048576 | tf_op jit(solution)/shard_map/all_to_all | solution.py:77
  23.5 17.4 %all-to-all-start = ((bf16[512,4,128]{0,2,1:T(8,128)(2,1)}), bf16[512,4,128]{0,2,1:T(8,128)(2,1)S(1)}, u32[]{:S(2)}, u32[]{:S(2)}) async-start(bf16[512,4,128]{0,2,1:T(8,128)(2,1)} %bitcast), calls=%async_computation | async-start | bytes 1048576 | tf_op jit(solution)/shard_map/all_to_all | solution.py:76
  26.9 14.0 %copy-start.26 = (bf16[1,512,128]{2,1,0:T(8,128)(2,1)S(1)}, bf16[1,512,128]{2,1,0:T(8,128)(2,1)}, u32[]{:S(2)}) copy-start(bf16[1,512,128]{2,1,0:T(8,128)(2,1)} %param.31) | copy-start | bytes 393220
  30.8 17.1 %copy-start.3 = (f32[512,4,128]{2,0,1:T(8,128)}, f32[512,4,128]{2,0,1:T(8,128)S(1)}, u32[]{:S(2)}) copy-start(f32[512,4,128]{2,0,1:T(8,128)S(1)} %convert_element_type.405) | copy-start | bytes 3145732
  41.8 5.7 %copy-start.32 = (f32[128]{0:T(128)S(1)}, f32[128]{0:T(128)}, u32[]{:S(2)}) copy-start(f32[128]{0:T(128)} %param.32) | copy-start | bytes 1540
  41.8 18.3 %all-to-all-start.2 = ((bf16[512,4,128]{2,0,1:T(8,128)(2,1)}), bf16[512,4,128]{2,0,1:T(8,128)(2,1)}, u32[]{:S(2)}, u32[]{:S(2)}) async-start(bf16[512,4,128]{2,0,1:T(8,128)(2,1)} %broadcast_in_dim.29), calls=%async_computation.2 | async-start | bytes 1048576 | tf_op jit(solution)/shard_map/all_to_all | solution.py:78
  46.3 3.0 %copy-start.15 = (bf16[512,4,128]{2,0,1:T(8,128)(2,1)}, bf16[512,4,128]{2,0,1:T(8,128)(2,1)S(1)}, u32[]{:S(2)}) copy-start(bf16[512,4,128]{2,0,1:T(8,128)(2,1)S(1)} %copy.49) | copy-start | bytes 1572868
  47.9 4.5 %copy-start.19 = (bf16[1,2048,1,128]{3,1,2,0:T(8,128)(2,1)}, bf16[1,2048,1,128]{3,1,2,0:T(8,128)(2,1)S(1)}, u32[]{:S(2)}) copy-start(bf16[1,2048,1,128]{3,1,2,0:T(8,128)(2,1)S(1)} %multiply_convert_fusion.2) | copy-start | bytes 1572868
  52.4 2.4 %copy-start.12 = (bf16[1,512,1024]{2,1,0:T(8,128)(2,1)}, bf16[1,512,1024]{2,1,0:T(8,128)(2,1)S(1)}, u32[]{:S(2)}) copy-start(bf16[1,512,1024]{2,1,0:T(8,128)(2,1)S(1)} %fusion.50) | copy-start | bytes 3145732
  53.9 1.9 %copy-start.7 = (bf16[1,512,1536]{2,1,0:T(8,128)(2,1)}, bf16[1,512,1536]{2,1,0:T(8,128)(2,1)S(1)}, u32[]{:S(2)}) copy-start(bf16[1,512,1536]{2,1,0:T(8,128)(2,1)S(1)} %fusion.27) | copy-start | bytes 4718596
  57.7 28.9 %copy-start.56 = (f32[128,4]{0,1:T(4,128)S(1)}, f32[128,4]{0,1:T(4,128)}, u32[]{:S(2)}) copy-start(f32[128,4]{0,1:T(4,128)} %param.37) | copy-start | bytes 6148
  88.6 19.3 %copy-start.52 = (f32[128]{0:T(128)}, f32[128]{0:T(128)S(1)}, u32[]{:S(2)}) copy-start(f32[128]{0:T(128)S(1)} %get-tuple-element.139) | copy-start | bytes 1540
  88.6 19.3 %copy-start.54 = (f32[128]{0:T(128)}, f32[128]{0:T(128)S(1)}, u32[]{:S(2)}) copy-start(f32[128]{0:T(128)S(1)} %get-tuple-element.141) | copy-start | bytes 1540
  94.1 9.7 %copy-start.46 = (f32[4]{0:T(128)}, f32[4]{0:T(128)S(1)}, u32[]{:S(2)}) copy-start(f32[4]{0:T(128)S(1)} %get-tuple-element.142) | copy-start | bytes 52
  94.1 9.7 %copy-start.48 = (f32[4]{0:T(128)}, f32[4]{0:T(128)S(1)}, u32[]{:S(2)}) copy-start(f32[4]{0:T(128)S(1)} %get-tuple-element.143) | copy-start | bytes 52
  105.1 3.1 %copy-start.27 = (bf16[1,2560]{1,0:T(2,128)(2,1)}, bf16[1,2560]{1,0:T(2,128)(2,1)S(1)}, u32[]{:S(2)}) copy-start(bf16[1,2560]{1,0:T(2,128)(2,1)S(1)} %subtract_multiply_fusion) | copy-start | bytes 15364
  105.1 3.1 %copy-start.24 = (bf16[1,2048,1,128]{3,1,2,0:T(8,128)(2,1)S(1)}, bf16[1,2048,1,128]{3,1,2,0:T(8,128)(2,1)}, u32[]{:S(2)}) copy-start(bf16[1,2048,1,128]{3,1,2,0:T(8,128)(2,1)} %copy-done.23) | copy-start | bytes 1572868
  108.0 8.4 %copy-start.31 = (f32[1,1024]{1,0:T(1,128)}, f32[1,1024]{1,0:T(1,128)S(1)}, u32[]{:S(2)}) copy-start(f32[1,1024]{1,0:T(1,128)S(1)} %slice.263) | copy-start | bytes 12292
  108.6 8.5 %copy-start.16 = (f32[128,512]{1,0:T(8,128)}, f32[128,512]{1,0:T(8,128)S(1)}, u32[]{:S(2)}) copy-start(f32[128,512]{1,0:T(8,128)S(1)} %fusion.60) | copy-start | bytes 786436
  112.6 2.6 %copy-start.1 = (bf16[512,2048]{1,0:T(8,128)(2,1)}, bf16[512,2048]{1,0:T(8,128)(2,1)S(1)}, u32[]{:S(2)}) copy-start(bf16[512,2048]{1,0:T(8,128)(2,1)S(1)} %fusion.22) | copy-start | bytes 6291460
  112.6 2.2 %copy-start.8 = (bf16[1,512,1536]{2,1,0:T(8,128)(2,1)S(1)}, bf16[1,512,1536]{2,1,0:T(8,128)(2,1)}, u32[]{:S(2)}) copy-start(bf16[1,512,1536]{2,1,0:T(8,128)(2,1)} %copy-done.7) | copy-start | bytes 4718596
  112.6 2.6 %copy-start.13 = (bf16[1,512,1024]{2,1,0:T(8,128)(2,1)S(1)}, bf16[1,512,1024]{2,1,0:T(8,128)(2,1)}, u32[]{:S(2)}) copy-start(bf16[1,512,1024]{2,1,0:T(8,128)(2,1)} %copy-done.12) | copy-start | bytes 3145732
  117.9 3.7 %copy-start.10 = (f32[512,4,128]{2,0,1:T(8,128)S(1)}, f32[512,4,128]{2,0,1:T(8,128)}, u32[]{:S(2)}) copy-start(f32[512,4,128]{2,0,1:T(8,128)} %copy-done.9) | copy-start | bytes 3145732
  124.5 9.2 %copy-start.6 = (f32[512,4,128]{2,0,1:T(8,128)S(1)}, f32[512,4,128]{2,0,1:T(8,128)}, u32[]{:S(2)}) copy-start(f32[512,4,128]{2,0,1:T(8,128)} %copy-done.3) | copy-start | bytes 3145732
  127.4 7.6 %copy-start.25 = (f32[512,1,128]{0,2,1:T(8,128)S(1)}, f32[512,1,128]{0,2,1:T(8,128)}, u32[]{:S(2)}) copy-start(f32[512,1,128]{0,2,1:T(8,128)} %convolution_bitcast_fusion.3) | copy-start | bytes 786436
  129.5 26.7 %all-to-all-start.3 = ((bf16[4,512,128]{1,2,0:T(8,128)(2,1)}), bf16[4,512,128]{1,2,0:T(8,128)(2,1)}, u32[]{:S(2)}, u32[]{:S(2)}) async-start(bf16[4,512,128]{1,2,0:T(8,128)(2,1)} %copy.54), calls=%async_computation.3 | async-start | bytes 1048576 | tf_op jit(solution)/shard_map/all_to_all | solution.py:253
  135.0 2.1 %copy-start.20 = (bf16[1,2048,1,128]{3,1,2,0:T(8,128)(2,1)S(1)}, bf16[1,2048,1,128]{3,1,2,0:T(8,128)(2,1)}, u32[]{:S(2)}) copy-start(bf16[1,2048,1,128]{3,1,2,0:T(8,128)(2,1)} %copy-done.19) | copy-start | bytes 1572868
  135.0 2.1 %copy-start.41 = (f32[512]{0:T(512)S(1)}, f32[512]{0:T(512)}, u32[]{:S(2)}) copy-start(f32[512]{0:T(512)} %copy-done.40) | copy-start | bytes 6148
  135.0 2.1 %copy-start.44 = (f32[512]{0:T(512)S(1)}, f32[512]{0:T(512)}, u32[]{:S(2)}) copy-start(f32[512]{0:T(512)} %get-tuple-element.154) | copy-start | bytes 6148
  137.2 1.8 %copy-start.14 = (f32[2048,1,128]{0,2,1:T(8,128)S(1)}, f32[2048,1,128]{0,2,1:T(8,128)}, u32[]{:S(2)}) copy-start(f32[2048,1,128]{0,2,1:T(8,128)} %copy.63) | copy-start | bytes 3145732
  139.7 5.1 %copy-start.29 = (f32[2048]{0:T(1024)S(1)}, f32[2048]{0:T(1024)}, u32[]{:S(2)}) copy-start(f32[2048]{0:T(1024)} %get-tuple-element.171) | copy-start | bytes 24580
  139.7 5.1 %copy-start.39 = (bf16[128]{0:T(256)(128)(2,1)S(1)}, bf16[128]{0:T(256)(128)(2,1)}, u32[]{:S(2)}) copy-start(bf16[128]{0:T(256)(128)(2,1)} %copy-done.38) | copy-start | bytes 772
  139.7 10.1 %copy-start.28 = (bf16[1,2560]{1,0:T(2,128)(2,1)S(1)}, bf16[1,2560]{1,0:T(2,128)(2,1)}, u32[]{:S(2)}) copy-start(bf16[1,2560]{1,0:T(2,128)(2,1)} %copy-done.27) | copy-start | bytes 15364
  139.7 15.3 %copy-start.37 = (f32[128]{0:T(128)S(1)}, f32[128]{0:T(128)}, u32[]{:S(2)}) copy-start(f32[128]{0:T(128)} %copy-done.36) | copy-start | bytes 1540
  139.9 21.3 %copy-start.51 = (f32[128]{0:T(128)S(1)}, f32[128]{0:T(128)}, u32[]{:S(2)}) copy-start(f32[128]{0:T(128)} %get-tuple-element.137) | copy-start | bytes 1540
  139.9 21.3 %copy-start.53 = (f32[128]{0:T(128)S(1)}, f32[128]{0:T(128)}, u32[]{:S(2)}) copy-start(f32[128]{0:T(128)} %copy-done.52) | copy-start | bytes 1540
  139.9 21.3 %copy-start.55 = (f32[128]{0:T(128)S(1)}, f32[128]{0:T(128)}, u32[]{:S(2)}) copy-start(f32[128]{0:T(128)} %copy-done.54) | copy-start | bytes 1540
  140.0 23.0 %copy-start.47 = (f32[4]{0:T(128)S(1)}, f32[4]{0:T(128)}, u32[]{:S(2)}) copy-start(f32[4]{0:T(128)} %copy-done.46) | copy-start | bytes 52
  140.0 23.0 %copy-start.49 = (f32[4]{0:T(128)S(1)}, f32[4]{0:T(128)}, u32[]{:S(2)}) copy-start(f32[4]{0:T(128)} %copy-done.48) | copy-start | bytes 52
  140.0 23.0 %copy-start.50 = (f32[4]{0:T(128)S(1)}, f32[4]{0:T(128)}, u32[]{:S(2)}) copy-start(f32[4]{0:T(128)} %get-tuple-element.144) | copy-start | bytes 52
  140.3 23.2 %collective-permute-start.2 = (bf16[512,128]{1,0:T(8,128)(2,1)S(1)}, bf16[512,128]{1,0:T(8,128)(2,1)S(1)}, u32[]{:S(2)}, u32[]{:S(2)}) collective-permute-start(bf16[512,128]{1,0:T(8,128)(2,1)S(1)} %get-tuple-element.146), channel_id=1, source_target_pairs={{0,12},{4,8},{8,4},{12,0},{1,13},{5,9},{9,5},{13,1},{2,14},{6,10},... | collective-permute-start | bytes 393224 | tf_op jit(solution)/shard_map/ppermute | solution.py:30
  144.2 19.4 %collective-permute-start.1 = (bf16[512,128]{1,0:T(8,128)(2,1)S(1)}, bf16[512,128]{1,0:T(8,128)(2,1)S(1)}, u32[]{:S(2)}, u32[]{:S(2)}) collective-permute-start(bf16[512,128]{1,0:T(8,128)(2,1)S(1)} %get-tuple-element.147), channel_id=1, source_target_pairs={{0,8},{4,12},{8,0},{12,4},{1,9},{5,13},{9,1},{13,5},{2,10},{6,14},... | collective-permute-start | bytes 393224 | tf_op jit(solution)/shard_map/ppermute | solution.py:30
  144.2 19.4 %collective-permute-start = (bf16[512,128]{1,0:T(8,128)(2,1)S(1)}, bf16[512,128]{1,0:T(8,128)(2,1)S(1)}, u32[]{:S(2)}, u32[]{:S(2)}) collective-permute-start(bf16[512,128]{1,0:T(8,128)(2,1)S(1)} %get-tuple-element.148), channel_id=1, source_target_pairs={{0,4},{4,0},{8,12},{12,8},{1,5},{5,1},{9,13},{13,9},{2,6},{6,2},{1... | collective-permute-start | bytes 393224 | tf_op jit(solution)/shard_map/ppermute | solution.py:30
  156.2 20.0 %all-to-all-start.4 = ((bf16[4,512,128]{2,1,0:T(8,128)(2,1)}), bf16[4,512,128]{2,1,0:T(8,128)(2,1)S(1)}, u32[]{:S(2)}, u32[]{:S(2)}) async-start(bf16[4,512,128]{2,1,0:T(8,128)(2,1)} %multiply_convert_fusion), calls=%async_computation.4 | async-start | bytes 1048576 | tf_op jit(solution)/shard_map/all_to_all | solution.py:255
  (18 other events, 19.5 us)
